TPU v7x, 32 devices: a whole 2x2x4 slice. The times are simulated.
32 devices in a mesh: replica: 16 (over z, y, x), shard: 2 (over core).
Axes of the slice: x: 2, y: 2, z: 4, core: 2. Of those that a mesh axis runs over, the one named last changes fastest.
Arguments:
- grad_query: float32 [32, 512, 384], P(('replica', 'shard')), may hold values from -0.3 to 0.3
- grad_output: float32 [32, 384, 512], P(('replica', 'shard')), may hold values from -0.3 to 0.3
- grad_norm: float32 [32, 512], P(('replica', 'shard')), may hold values from -0.3 to 0.3
- grad_bias: float32 [32, 32, 6], P(('replica', 'shard')), may hold values from -0.3 to 0.3
- weight_query: float32 [512, 384], P('shard'), may hold values from -5.303301 to 5.303301
- weight_output: float32 [384, 512], P('shard'), may hold values from -6.1237244 to 6.1237244
- weight_norm: float32 [512], P('shard'), may hold values from 0 to 120
- weight_bias: float32 [32, 6], P('shard'), may hold values from -120 to 120
- first_query: float32 [512, 384], P('shard'), may hold values from -120 to 120
- first_output: float32 [384, 512], P('shard'), may hold values from -120 to 120
- first_norm: float32 [512], P('shard'), may hold values from -120 to 120
- first_bias: float32 [32, 6], P('shard'), may hold values from -120 to 120
- second_query: float32 [512, 384], P('shard'), may hold values from 0.05 to 2
- second_output: float32 [384, 512], P('shard'), may hold values from 0.05 to 2
- second_norm: float32 [512], P('shard'), may hold values from 0.05 to 2
- second_bias: float32 [32, 6], P('shard'), may hold values from 0.05 to 2
Outputs:
- updated_query: bfloat16 [512, 384], replicated
- updated_output: bfloat16 [384, 512], replicated
- updated_norm: bfloat16 [512], replicated
- updated_bias: bfloat16 [32, 6], replicated
- first_query_next: float32 [512, 384], P('shard')
- first_output_next: float32 [384, 512], P('shard')
- first_norm_next: float32 [512], P('shard')
- first_bias_next: float32 [32, 6], P('shard')
- second_query_next: float32 [512, 384], P('shard')
- second_output_next: float32 [384, 512], P('shard')
- second_norm_next: float32 [512], P('shard')
- second_bias_next: float32 [32, 6], P('shard')
- norm_table: float32 [2, 4], replicated
- trust_ratios: float32 [4], replicated
All inputs are finite; a program needn't handle non-finite values.
Results may differ from a plain program's by a relative error of at most 0.008.
Values may be sent and summed in bfloat16 or wider, within the bound.
A program may use at most 64 MiB of HBM per device.

v0:
```python
import jax
import jax.numpy as jnp
from jax import lax
from jax.sharding import PartitionSpec as P


def step_math(summed, moment, second, weight, decay_rate):
    moment_next = 0.5 * moment + 0.5 * summed
    second_next = 0.5 * second + 0.5 * summed * summed
    update = moment_next / (jnp.sqrt(second_next) + 1e-06) + decay_rate * weight
    return (moment_next, second_next, update)


def on_device(
    grad_query,
    grad_output,
    grad_norm,
    grad_bias,
    weight_query,
    weight_output,
    weight_norm,
    weight_bias,
    first_query,
    first_output,
    first_norm,
    first_bias,
    second_query,
    second_output,
    second_norm,
    second_bias,
):
    weights = (weight_query, weight_output, weight_norm, weight_bias)
    moments = (first_query, first_output, first_norm, first_bias)
    seconds = (second_query, second_output, second_norm, second_bias)
    decay_rates = (0.01, 0.01, 0.0, 0.0)
    gradients = (grad_query[0], grad_output[0], grad_norm[0], grad_bias[0])
    totals = lax.psum(
        (gradients[0], gradients[1], gradients[2], gradients[3]), ("replica", "shard")
    )
    position = lax.axis_index("shard")
    summed_all = tuple(
        (
            lax.dynamic_slice_in_dim(entire, position * weight.shape[0], weight.shape[0], 0)
            for entire, weight in zip(totals, weights)
        )
    )
    results = [
        step_math(
            summed_all[member],
            moments[member],
            seconds[member],
            weights[member],
            decay_rates[member],
        )
        for member in range(4)
    ]
    weight_squares = [jnp.sum(weight * weight) for weight in weights]
    update_squares = [jnp.sum(result[2] * result[2]) for result in results]
    couples = [
        lax.psum((weight_squares[member], update_squares[member]), "shard") for member in range(4)
    ]
    weight_sizes = jnp.sqrt(jnp.stack([couple[0] for couple in couples]))
    update_sizes = jnp.sqrt(jnp.stack([couple[1] for couple in couples]))
    trust_ratios = weight_sizes / (update_sizes + 1e-06)
    shards = tuple(
        (
            (weights[member] - 0.01 * trust_ratios[member] * results[member][2]).astype(
                jnp.bfloat16
            )
            for member in range(4)
        )
    )
    gathered = (
        lax.all_gather(shards[0], "shard", axis=0, tiled=True),
        lax.all_gather(shards[1], "shard", axis=0, tiled=True),
        lax.all_gather(shards[2], "shard", axis=0, tiled=True),
        lax.all_gather(shards[3], "shard", axis=0, tiled=True),
    )
    norm_table = jnp.stack([weight_sizes, update_sizes])
    return (
        gathered[0],
        gathered[1],
        gathered[2],
        gathered[3],
        results[0][0],
        results[1][0],
        results[2][0],
        results[3][0],
        results[0][1],
        results[1][1],
        results[2][1],
        results[3][1],
        norm_table,
        trust_ratios,
    )


def solution(mesh):
    placed = (
        P(("replica", "shard"), None, None),
        P(("replica", "shard"), None, None),
        P(("replica", "shard"), None),
        P(("replica", "shard"), None, None),
        P("shard", None),
        P("shard", None),
        P("shard"),
        P("shard", None),
        P("shard", None),
        P("shard", None),
        P("shard"),
        P("shard", None),
        P("shard", None),
        P("shard", None),
        P("shard"),
        P("shard", None),
    )
    return jax.shard_map(
        on_device,
        mesh=mesh,
        in_specs=placed,
        out_specs=(
            P(),
            P(),
            P(),
            P(),
            P("shard", None),
            P("shard", None),
            P("shard"),
            P("shard", None),
            P("shard", None),
            P("shard", None),
            P("shard"),
            P("shard", None),
            P(),
            P(),
        ),
        check_vma=False,
    )
```

profile of v0, /device:TPU:0, one launch (start us, length us, event | category | flops | bytes accessed | tf_op | source)
XLA Modules:
  0.0 187.0 jit_solution(17998215952800912124)
XLA Ops:
  7.2 0.0 all-reduce.5.cloned.1.call-start
  7.3 0.7 all-reduce.5.cloned.1.call-update
  7.9 0.7 copy-done.18
  8.6 0.0 copy-start.19
  8.6 0.7 copy-done.19
  9.3 42.5 %all-reduce = (f32[32,6]{0,1:T(8,128)S(1)}, f32[512]{0:T(512)S(1)}) all-reduce(f32[32,6]{0,1:T(8,128)S(1)} %bitcast.34, f32[512]{0:T(512)S(1)} %bitcast.36), channel_id=1, replica_groups=mesh['replica'=16,'shard'=2] {'replica','shard'}, use_global_device_ids=true, to_apply=%region_17.0 | all-reduce | flops 704 | bytes 5632 | tf_op jit(solution)/shard_map/psum | solution.py:37
  51.8 0.0 copy-done.20
  51.8 0.0 copy-start.11
  51.8 0.0 copy-start.15
  51.8 1.3 multiply_reduce_fusion.6
  53.1 0.7 multiply_reduce_fusion.4
  53.8 95.0 %all-reduce.5.cloned.1.call-done = (f32[384,512]{1,0:T(8,128)}, f32[512,384]{1,0:T(8,128)}) async-done(((f32[384,512]{1,0:T(8,128)}, f32[512,384]{1,0:T(8,128)}), (f32[384,512]{1,0:T(8,128)}, f32[512,384]{1,0:T(8,128)})) %all-reduce.5.cloned.1.call-update) | async-done | bytes 1572880 | tf_op jit(solution)/shard_map/psum | solution.py:37
  148.8 0.0 copy-start.8
  148.8 0.0 copy-start.9
  148.8 2.1 %multiply_reduce_fusion.1 = (f32[]{:T(128)}, f32[]{:T(128)}, f32[256,384]{1,0:T(8,128)S(1)}, f32[256,384]{1,0:T(8,128)S(1)}) fusion(f32[256,384]{1,0:T(8,128)S(1)} %copy-done.1, f32[512,384]{1,0:T(8,128)} %get-tuple-element.23, s32[]{:T(128)S(6)} %select_n.10, f32[256,384]{1,0:T(8,128)S(1)} %copy-done.6, f32[256,384]{1,0:T(8,128)S(1)} %copy-done.7), kind=kLoop, calls=%fused_computation.10 | loop fusion | flops 1376254 | bytes 2359308 | tf_op jit(solution)/shard_map/reduce_sum | solution.py:58
  151.0 1.0 multiply_reduce_fusion
  152.0 3.2 %all-reduce.2 = (f32[]{:T(128)}, f32[]{:T(128)}, f32[]{:T(128)}, f32[]{:T(128)}, f32[]{:T(128)}, /*index=5*/f32[]{:T(128)}, f32[]{:T(128)}, f32[]{:T(128)}) all-reduce(f32[]{:T(128)} %get-tuple-element.19, f32[]{:T(128)} %get-tuple-element.42, f32[]{:T(128)} %get-tuple-element.17, ...), channel_id=1, replica_groups=mesh['replica'=16,'shard'=2] {'shard'}, use_global_device_ids=true, to_apply=%region_7.0 | all-reduce | flops 8 | bytes 64 | tf_op jit(solution)/shard_map/psum | solution.py:60
  155.2 5.1 %fusion.5 = f32[4]{0:T(128)S(1)} fusion(f32[1]{0:T(128)} %bitcast.3, f32[1]{0:T(128)} %bitcast.2, f32[1]{0:T(128)} %bitcast.1, f32[1]{0:T(128)} %bitcast, f32[1]{0:T(128)} %bitcast.10, f32[1]{0:T(128)} %bitcast.9, f32[1]{0:T(128)} %bitcast.7, f32[1]{0:T(128)} %bitcast.5), kind=kLoop, calls=%fused_computation.32 | loop fusion | flops 32 | bytes 48 | tf_op jit(solution)/shard_map/div | solution.py:64
  160.3 0.0 copy-start.14
  160.3 0.6 fusion.11
  161.6 0.2 subtract_convert_fusion
  161.8 2.1 %all_gather.13 = bf16[384,512]{1,0:T(8,128)(2,1)S(1)} all-gather(bf16[192,512]{1,0:T(8,128)(2,1)S(1)} %subtract_convert_fusion), channel_id=1, replica_groups=mesh['replica'=16,'shard'=2] {'shard'}, dimensions={0}, use_global_device_ids=true | all-gather | bytes 589824 | tf_op jit(solution)/shard_map/all_gather | solution.py:75
  164.5 0.2 subtract_convert_fusion.1
  164.7 2.1 %all_gather.12 = bf16[512,384]{1,0:T(8,128)(2,1)S(1)} all-gather(bf16[256,384]{1,0:T(8,128)(2,1)S(1)} %subtract_convert_fusion.1), channel_id=1, replica_groups=mesh['replica'=16,'shard'=2] {'shard'}, dimensions={0}, use_global_device_ids=true | all-gather | bytes 589824 | tf_op jit(solution)/shard_map/all_gather | solution.py:74
  167.5 1.8 all-gather.1
  169.3 0.7 reshape.157
  170.6 1.8 all-gather
  172.4 0.6 copy.33
  173.0 5.1 %maximum_sqrt_fusion.2 = (f32[1,4]{1,0:T(1,128)S(1)}, f32[1,4]{1,0:T(1,128)S(1)}) fusion(f32[1,1]{1,0:T(1,128)} %bitcast.19, f32[1,1]{1,0:T(1,128)} %bitcast.18, f32[1,1]{1,0:T(1,128)} %bitcast.17, f32[1,1]{1,0:T(1,128)} %bitcast.16, f32[1,1]{1,0:T(1,128)} %bitcast.23, f32[1,1]{1,0:T(1,128)} %bitcast.22, f32[1,1]{1,0:T(1,128)} %bitcast.21, f32[1,1]{1,0:T(1,128)} %bitcast.20), kind=kLoop, calls=%fused_computation.35 | loop fusion | flops 24 | bytes 64 | tf_op jit(solution)/shard_map/sqrt | solution.py:62
  178.1 0.6 pad_maximum_fusion
  178.7 0.7 copy.42
  179.4 0.7 copy.43
  (41 shorter events, 0.1 us)
Async XLA Ops:
  7.2 141.6 %all-reduce.5.cloned.1.call-start = ((), (), s32[]{:S(2)}) async-start(), calls=%async_computation | async-start | bytes 3145728 | tf_op jit(solution)/shard_map/psum | solution.py:37
  7.2 141.6 %copy-start.1 = (f32[256,384]{1,0:T(8,128)S(1)}, f32[256,384]{1,0:T(8,128)}, u32[]{:S(2)}) copy-start(f32[256,384]{1,0:T(8,128)} %param.20) | copy-start | bytes 1179652
  7.2 141.6 %copy-start.6 = (f32[256,384]{1,0:T(8,128)S(1)}, f32[256,384]{1,0:T(8,128)}, u32[]{:S(2)}) copy-start(f32[256,384]{1,0:T(8,128)} %param.28) | copy-start | bytes 1179652
  7.2 141.6 %copy-start.7 = (f32[256,384]{1,0:T(8,128)S(1)}, f32[256,384]{1,0:T(8,128)}, u32[]{:S(2)}) copy-start(f32[256,384]{1,0:T(8,128)} %param.24) | copy-start | bytes 1179652
  7.9 0.7 copy-start.18
  8.6 43.2 %copy-start.17 = (f32[256]{0:T(256)S(1)}, f32[256]{0:T(256)}, u32[]{:S(2)}) copy-start(f32[256]{0:T(256)} %param.22) | copy-start | bytes 3076
  8.6 43.2 %copy-start.20 = (f32[256]{0:T(256)S(1)}, f32[256]{0:T(256)}, u32[]{:S(2)}) copy-start(f32[256]{0:T(256)} %param.30) | copy-start | bytes 3076
  8.6 43.2 %copy-start.21 = (f32[256]{0:T(256)S(1)}, f32[256]{0:T(256)}, u32[]{:S(2)}) copy-start(f32[256]{0:T(256)} %param.26) | copy-start | bytes 3076
  8.6 0.7 copy-start.19
  51.8 1.3 copy-start.16
  51.8 1.3 copy-start.11
  51.8 1.3 copy-start.15
  53.8 113.6 %copy-start.12 = (f32[16,6]{0,1:T(8,128)}, f32[16,6]{0,1:T(8,128)S(1)}, u32[]{:S(2)}) copy-start(f32[16,6]{0,1:T(8,128)S(1)} %get-tuple-element.74) | copy-start | bytes 1156
  53.8 113.6 %copy-start.13 = (f32[16,6]{0,1:T(8,128)}, f32[16,6]{0,1:T(8,128)S(1)}, u32[]{:S(2)}) copy-start(f32[16,6]{0,1:T(8,128)S(1)} %get-tuple-element.70) | copy-start | bytes 1156
  148.8 2.2 %copy-start = (f32[192,512]{1,0:T(8,128)S(1)}, f32[192,512]{1,0:T(8,128)}, u32[]{:S(2)}) copy-start(f32[192,512]{1,0:T(8,128)} %param.21) | copy-start | bytes 1179652
  148.8 2.1 %copy-start.8 = (f32[192,512]{1,0:T(8,128)S(1)}, f32[192,512]{1,0:T(8,128)}, u32[]{:S(2)}) copy-start(f32[192,512]{1,0:T(8,128)} %param.29) | copy-start | bytes 1179652
  148.8 2.1 %copy-start.9 = (f32[192,512]{1,0:T(8,128)S(1)}, f32[192,512]{1,0:T(8,128)}, u32[]{:S(2)}) copy-start(f32[192,512]{1,0:T(8,128)} %param.25) | copy-start | bytes 1179652
  148.8 2.1 %copy-start.10 = (f32[384,512]{1,0:T(8,128)S(1)}, f32[384,512]{1,0:T(8,128)}, u32[]{:S(2)}) copy-start(f32[384,512]{1,0:T(8,128)} %get-tuple-element.22) | copy-start | bytes 2359300
  150.9 13.5 %copy-start.2 = (f32[256,384]{1,0:T(8,128)}, f32[256,384]{1,0:T(8,128)S(1)}, u32[]{:S(2)}) copy-start(f32[256,384]{1,0:T(8,128)S(1)} %get-tuple-element.71) | copy-start | bytes 1179652
  150.9 13.5 %copy-start.3 = (f32[256,384]{1,0:T(8,128)}, f32[256,384]{1,0:T(8,128)S(1)}, u32[]{:S(2)}) copy-start(f32[256,384]{1,0:T(8,128)S(1)} %get-tuple-element.67) | copy-start | bytes 1179652
  152.0 9.8 %copy-start.4 = (f32[192,512]{1,0:T(8,128)}, f32[192,512]{1,0:T(8,128)S(1)}, u32[]{:S(2)}) copy-start(f32[192,512]{1,0:T(8,128)S(1)} %get-tuple-element.72) | copy-start | bytes 1179652
  152.0 9.8 %copy-start.5 = (f32[192,512]{1,0:T(8,128)}, f32[192,512]{1,0:T(8,128)S(1)}, u32[]{:S(2)}) copy-start(f32[192,512]{1,0:T(8,128)S(1)} %get-tuple-element.68) | copy-start | bytes 1179652
  160.3 0.6 copy-start.14
Sparse Core Ops, SparseCore 0:
  13.5 135.2 all-reduce.4
where the time goes:
time: 188 us; the launch traced here: 187 us
  waiting for transfers between devices  95.6 us (51%)
  blocking collectives  53.4 us (28%)
  between operations  16.8 us (9%)
  other arithmetic  16.4 us (9%)
  local copies, waits for them, and re-layouts  4.81 us (3%)
    psum x1, waiting for transfers between devices, on_device(): lax.psum((gradients[0], gradients[1], gradients[2], gradients[3]), ('repl...  95 us
    psum x1, blocking collectives, on_device(): lax.psum((gradients[0], gradients[1], gradients[2], gradients[3]), ('repl...  42.5 us
    div x1, other arithmetic, on_device(): trust_ratios = weight_sizes / (update_sizes + 1e-06)  5.14 us
    sqrt x1, other arithmetic, on_device(): weight_sizes = jnp.sqrt(jnp.stack([couple[0] for couple in couples]))  5.13 us
    reduce_sum x4, other arithmetic, on_device(): update_squares = [jnp.sum(result[2] * result[2]) for result in results]  5.08 us
    unnamed x50, local copies, waits for them, and re-layouts  4.21 us
  transfers between devices with their start and end apart: 1, of which 1 were waited for; matrix products, arithmetic and copies ran while one was open for 1% of the time, Pallas kernels for 0%

commit v1 on v0

v1 whole, which is shorter than its diff:
```python
import functools

import jax
import jax.numpy as jnp
from jax import lax
from jax.experimental import pallas as pl
from jax.experimental.pallas import tpu as pltpu
from jax.sharding import PartitionSpec as P

MESH = pl.DeviceIdType.MESH
LANES = 128
DECAY = 0.01


def up(value, step):
    return -(-value // step) * step


class Sizes:
    def __init__(self, shards, replicas, query, output, norm, bias):
        self.S, self.R = shards, replicas
        self.B = 4 if replicas % 4 == 0 else 1
        self.A = replicas // self.B
        self.n = (query[0], output[0])
        self.cols = (query[1], output[1])
        self.blocks = tuple(c // LANES for c in self.cols)
        self.used = tuple(n * j for n, j in zip(self.n, self.blocks))
        self.piece = tuple(up(-(-u // replicas), 16) for u in self.used)
        self.quarter = tuple(self.A * p for p in self.piece)
        self.total = tuple(replicas * p for p in self.piece)
        self.L = min(LANES, norm[0])
        self.q = norm[0] // self.L
        self.norm_rows = up(self.q * shards, 8)
        self.b, self.heads = bias
        self.small_rows = up(self.norm_rows + self.b * shards, 8)
        self.state_norm = up(3 * self.q, 8)
        self.bp = up(self.b, 8)
        self.state_rows = self.state_norm + 3 * self.bp


def step_math(summed, moment, second):
    moment_next = 0.5 * moment + 0.5 * summed
    second_next = 0.5 * second + 0.5 * summed * summed
    return moment_next, second_next, moment_next / (jnp.sqrt(second_next) + 1e-06)


def exchange_kernel(
    z,
    gq, go, gn, gb, wq, wo, wn, wb, fq, fo, fn, fb, sq, so, sn, sb,
    fin_q, fin_o, u_q, u_o, full_q, full_o, small_out, state, sums,
    core_q, core_o, acc_q, acc_o, send_q, send_o, plane_q, plane_o,
    quarter_q, quarter_o, zsend_q, zsend_o, zin_q, zin_o,
    wv_q, wv_o, fv_q, fv_o, sv_q, sv_o, small_core, small_plane, small_z,
    shard_send, shard_recv, plane_send, plane_recv, z_send, z_recv, local,
):
    S, B, A = z.S, z.B, z.A
    s = lax.axis_index("shard")
    r = lax.axis_index("replica")
    a, b = lax.div(r, B), lax.rem(r, B)
    grads, weights, firsts, seconds = (gq, go), (wq, wo), (fq, fo), (sq, so)
    fins, us, fulls = (fin_q, fin_o), (u_q, u_o), (full_q, full_o)
    cores, accs, sends, planes = (core_q, core_o), (acc_q, acc_o), (send_q, send_o), (plane_q, plane_o)
    quarters, zsends, zins = (quarter_q, quarter_o), (zsend_q, zsend_o), (zin_q, zin_o)
    wvs, fvs, svs = (wv_q, wv_o), (fv_q, fv_o), (sv_q, sv_o)
    started = []

    def shard_peer(d):
        return lax.rem(s + d, S)

    def plane_peer(d):
        return (a * B + lax.rem(b + d, B), s)

    def z_peer(d):
        return (lax.rem(a + d, A) * B + b, s)

    def go_to(src, dst, send, recv, device):
        copy = pltpu.make_async_remote_copy(
            src_ref=src, dst_ref=dst, send_sem=send, recv_sem=recv,
            device_id=device, device_id_type=MESH,
        )
        copy.start()
        started.append(copy)
        return copy

    def to_shard(kind, src_of, dst):
        return [
            go_to(src_of(shard_peer(d)), dst, shard_send.at[kind, d], shard_recv.at[kind, d], (r, shard_peer(d)))
            for d in range(1, S)
        ]

    def to_plane(kind, src_of, dst_of):
        return [
            go_to(src_of(lax.rem(b + d, B)), dst_of(d), plane_send.at[kind, d], plane_recv.at[kind, d], plane_peer(d))
            for d in range(1, B)
        ]

    def to_z(kind, src_of, dst_of):
        return [
            go_to(src_of(lax.rem(a + d, A)), dst_of(d), z_send.at[kind, d], z_recv.at[kind, d], z_peer(d))
            for d in range(1, A)
        ]

    def arrived(copies):
        for copy in copies:
            copy.wait_recv()

    def rows(index, count, step):
        return pl.ds(pl.multiple_of(index * count, step), count)

    own = []
    for c in range(2):
        copy = pltpu.make_async_copy(grads[c].at[0, rows(s, z.n[c], 8), :], cores[c].at[s], local.at[c])
        copy.start()
        own.append(copy)

    barrier = pltpu.get_barrier_semaphore()
    for d in range(1, S):
        pl.semaphore_signal(barrier, inc=1, device_id=(r, shard_peer(d)), device_id_type=MESH)
    for d in range(1, B):
        pl.semaphore_signal(barrier, inc=1, device_id=plane_peer(d), device_id_type=MESH)
    for d in range(1, A):
        pl.semaphore_signal(barrier, inc=1, device_id=z_peer(d), device_id_type=MESH)

    small_core[s] = jnp.zeros((z.small_rows, LANES), jnp.float32)
    for i in range(z.q * S):
        small_core[s, i : i + 1, : z.L] = gn[:, i * z.L : (i + 1) * z.L]
    small_core[s, z.norm_rows : z.norm_rows + z.b * S, : z.heads] = gb[0]
    state[s] = jnp.zeros((z.state_rows, LANES), jnp.float32)
    for t, ref in enumerate((wn, fn, sn)):
        for i in range(z.q):
            row = t * z.q + i
            state[s, row : row + 1, : z.L] = ref[:, i * z.L : (i + 1) * z.L]
    for t, ref in enumerate((wb, fb, sb)):
        row = z.state_norm + t * z.bp
        state[s, row : row + z.b, : z.heads] = ref[...]

    pl.semaphore_wait(barrier, S + B + A - 3)

    core_in = [
        to_shard(c, lambda peer, c=c: grads[c].at[0, rows(peer, z.n[c], 8), :], cores[c].at[s])
        for c in range(2)
    ]
    small_in = to_shard(2, lambda peer: small_core.at[s], small_core.at[s])
    held = []
    for c in range(2):
        for t, (src, dst) in enumerate(((weights[c], wvs[c]), (firsts[c], fvs[c]), (seconds[c], svs[c]))):
            copy = pltpu.make_async_copy(src, dst, local.at[2 + 3 * c + t])
            copy.start()
            held.append(copy)

    plane_in = []
    for c in range(2):
        own[c].wait()
        arrived(core_in[c])
        n = z.n[c]
        for j in range(z.blocks[c]):
            part = cores[c][0, :, j * LANES : (j + 1) * LANES]
            for k in range(1, S):
                part = part + cores[c][k, :, j * LANES : (j + 1) * LANES]
            accs[c][j * n : (j + 1) * n, :] = part
            sends[c][j * n : (j + 1) * n, :] = part.astype(jnp.bfloat16)
        if z.used[c] < z.total[c]:
            rest = (z.total[c] - z.used[c], LANES)
            accs[c][z.used[c] :, :] = jnp.zeros(rest, jnp.float32)
            sends[c][z.used[c] :, :] = jnp.zeros(rest, jnp.bfloat16)
        plane_in.append(
            to_plane(
                c,
                lambda peer, c=c: sends[c].at[rows(peer, z.quarter[c], 16), :],
                lambda d, c=c: planes[c].at[d - 1],
            )
        )
    arrived(small_in)
    small = small_core[0]
    for k in range(1, S):
        small = small + small_core[k]
    small_plane[b] = small
    small_in = to_plane(2, lambda peer: small_plane.at[b], lambda d: small_plane.at[b])

    late = []
    for c in range(2):
        late += to_shard(3 + c, lambda peer, c=c: weights[c], fulls[c].at[rows(s, z.n[c], 8), :])
        copy = pltpu.make_async_copy(weights[c], fulls[c].at[rows(s, z.n[c], 8), :], local.at[8 + c])
        copy.start()
        held.append(copy)
    late += to_shard(5, lambda peer: state.at[s], state.at[s])

    z_in = []
    for c in range(2):
        arrived(plane_in[c])
        part = accs[c][rows(b, z.quarter[c], 16), :]
        for d in range(1, B):
            part = part + planes[c][d - 1].astype(jnp.float32)
        quarters[c][...] = part
        zsends[c][...] = part.astype(jnp.bfloat16)
        z_in.append(
            to_z(
                c,
                lambda peer, c=c: zsends[c].at[rows(peer, z.piece[c], 16), :],
                lambda d, c=c: zins[c].at[d - 1],
            )
        )
    arrived(small_in)
    small = small_plane[0]
    for k in range(1, B):
        small = small + small_plane[k]
    small_z[a] = small
    small_in = to_z(2, lambda peer: small_z.at[a], lambda d: small_z.at[a])

    back_z = []
    for c in range(2):
        arrived(z_in[c])
        part = quarters[c][rows(a, z.piece[c], 16), :]
        for d in range(1, A):
            part = part + zins[c][d - 1].astype(jnp.float32)
        mine = rows(b * A + a, z.piece[c], 16)
        fins[c][mine, :] = part.astype(jnp.bfloat16)
        back_z.append(
            to_z(3 + c, lambda peer, c=c, mine=mine: fins[c].at[mine, :], lambda d, c=c, mine=mine: fins[c].at[mine, :])
        )

    back_plane = []
    for c in range(2):
        arrived(back_z[c])
        mine = rows(b, z.quarter[c], 16)
        back_plane.append(
            to_plane(3 + c, lambda peer, c=c, mine=mine: fins[c].at[mine, :], lambda d, c=c, mine=mine: fins[c].at[mine, :])
        )
    arrived(small_in)
    small = small_z[0]
    for k in range(1, A):
        small = small + small_z[k]
    small_out[...] = small
    for copy in held:
        copy.wait()
    sums[s] = jnp.zeros((8, LANES), jnp.float32)
    for c in range(2):
        squares = jnp.zeros((1, LANES), jnp.float32)
        for j in range(z.blocks[c]):
            weight = wvs[c][:, j * LANES : (j + 1) * LANES]
            squares = squares + jnp.sum(weight * weight, axis=0, keepdims=True)
        sums[s, 2 * c : 2 * c + 1, :] = squares

    for c in range(2):
        arrived(back_plane[c])
        n = z.n[c]
        mine = rows(s, n, 16)
        squares = jnp.zeros((1, LANES), jnp.float32)
        for j in range(z.blocks[c]):
            lanes = slice(j * LANES, (j + 1) * LANES)
            summed = fins[c][j * n : (j + 1) * n, :].astype(jnp.float32)
            _, _, update = step_math(summed, fvs[c][:, lanes], svs[c][:, lanes])
            update = update + DECAY * wvs[c][:, lanes]
            squares = squares + jnp.sum(update * update, axis=0, keepdims=True)
            us[c][mine, lanes] = update.astype(jnp.bfloat16)
        sums[s, 2 * c + 1 : 2 * c + 2, :] = squares
        late += to_shard(6 + c, lambda peer, c=c, mine=mine: us[c].at[mine, :], us[c].at[mine, :])
    late += to_shard(8, lambda peer: sums.at[s], sums.at[s])
    arrived(late)
    for copy in started:
        copy.wait_send()


def finish_kernel(
    z,
    fin_q, fin_o, u_q, u_o, full_q, full_o, small, state, sums, fq, fo, sq, so,
    new_q, new_o, new_n, new_b, fq_next, fo_next, fn_next, fb_next,
    sq_next, so_next, sn_next, sb_next, table, trust,
):
    S, L, h = z.S, z.L, z.heads
    s = lax.axis_index("shard")
    totals = sums[0]
    for k in range(1, S):
        totals = totals + sums[k]

    def whole(row):
        return jnp.sum(totals[row : row + 1, :], axis=1, keepdims=True)

    squares = [(whole(0), whole(1)), (whole(2), whole(3))]

    def norm_of(k):
        rows = [state[k, t * z.q : (t + 1) * z.q, :L] for t in range(3)]
        return small[pl.ds(k * z.q, z.q), :L], rows

    def bias_of(k):
        rows = [state[k, z.state_norm + t * z.bp : z.state_norm + t * z.bp + z.b, :h] for t in range(3)]
        return small[pl.ds(z.norm_rows + k * z.b, z.b), :h], rows

    def total(value):
        return jnp.sum(jnp.sum(value, axis=0, keepdims=True), axis=1, keepdims=True)

    pairs = []
    for part_of in (norm_of, bias_of):
        couples, wsum, usum = [], None, None
        for k in range(S):
            summed, (weight, moment, second) = part_of(k)
            update = step_math(summed, moment, second)[2]
            couples.append((weight, update))
            ws, us = total(weight * weight), total(update * update)
            wsum = ws if wsum is None else wsum + ws
            usum = us if usum is None else usum + us
        squares.append((wsum, usum))
        pairs.append(couples)

    wsizes = [jnp.sqrt(pair[0]) for pair in squares]
    usizes = [jnp.sqrt(pair[1]) for pair in squares]
    ratios = [w / (u + 1e-06) for w, u in zip(wsizes, usizes)]

    column = lax.broadcasted_iota(jnp.int32, (2, 4), 1)
    row = lax.broadcasted_iota(jnp.int32, (2, 4), 0)
    values = jnp.zeros((2, 4), jnp.float32)
    for k in range(4):
        values = jnp.where(column == k, jnp.where(row == 0, wsizes[k], usizes[k]), values)
    table[...] = values
    column = lax.broadcasted_iota(jnp.int32, (1, 4), 1)
    values = jnp.zeros((1, 4), jnp.float32)
    for k in range(4):
        values = jnp.where(column == k, ratios[k], values)
    trust[...] = values

    for k in range(S):
        weight, update = pairs[0][k]
        value = (weight - 0.01 * ratios[2] * update).astype(jnp.bfloat16)
        for i in range(z.q):
            at = (k * z.q + i) * L
            new_n[:, at : at + L] = value[i : i + 1, :]
        weight, update = pairs[1][k]
        new_b[k * z.b : (k + 1) * z.b, :] = (weight - 0.01 * ratios[3] * update).astype(jnp.bfloat16)
    summed, (_, moment, second) = norm_of(s)
    moment_next, second_next, _ = step_math(summed, moment, second)
    for i in range(z.q):
        fn_next[:, i * L : (i + 1) * L] = moment_next[i : i + 1, :]
        sn_next[:, i * L : (i + 1) * L] = second_next[i : i + 1, :]
    summed, (_, moment, second) = bias_of(s)
    moment_next, second_next, _ = step_math(summed, moment, second)
    fb_next[...] = moment_next
    sb_next[...] = second_next

    for c, (fin, u, full, first, second, new, first_next, second_next) in enumerate((
        (fin_q, u_q, full_q, fq, sq, new_q, fq_next, sq_next),
        (fin_o, u_o, full_o, fo, so, new_o, fo_next, so_next),
    )):
        n = z.n[c]
        for j in range(z.blocks[c]):
            lanes = slice(j * LANES, (j + 1) * LANES)
            summed = fin[j * n : (j + 1) * n, :].astype(jnp.float32)
            moment_value, second_value, _ = step_math(summed, first[:, lanes], second[:, lanes])
            first_next[:, lanes] = moment_value
            second_next[:, lanes] = second_value
        new[...] = (full[...] - 0.01 * ratios[c] * u[...].astype(jnp.float32)).astype(jnp.bfloat16)


def on_device(
    shards, replicas,
    gq, go, gn, gb, wq, wo, wn, wb, fq, fo, fn, fb, sq, so, sn, sb,
):
    f32, bf16 = jnp.float32, jnp.bfloat16
    z = Sizes(shards, replicas, wq.shape, wo.shape, wn.shape, wb.shape)
    S, B, A = z.S, z.B, z.A
    wn, fn, sn = (value.reshape(1, -1) for value in (wn, fn, sn))
    any_spec = pl.BlockSpec(memory_space=pl.ANY)
    vmem = pl.BlockSpec(memory_space=pltpu.VMEM)
    shape = jax.ShapeDtypeStruct
    whole = [(n * S, cols) for n, cols in zip(z.n, z.cols)]
    both = (0, 1)

    def scratch(shape_of, dtype):
        return [pltpu.VMEM(shape_of(c), dtype) for c in both]

    outs = pl.pallas_call(
        functools.partial(exchange_kernel, z),
        out_shape=[shape((z.total[c], LANES), bf16) for c in both]
        + [shape(whole[c], bf16) for c in both]
        + [shape(whole[c], f32) for c in both]
        + [shape((z.small_rows, LANES), f32), shape((S, z.state_rows, LANES), f32), shape((S, 8, LANES), f32)],
        in_specs=[any_spec, any_spec, vmem, vmem] + [any_spec, any_spec, vmem, vmem] * 3,
        out_specs=[vmem] * 4 + [any_spec] * 2 + [vmem] * 3,
        scratch_shapes=scratch(lambda c: (S, z.n[c], z.cols[c]), f32)
        + scratch(lambda c: (z.total[c], LANES), f32)
        + scratch(lambda c: (z.total[c], LANES), bf16)
        + scratch(lambda c: (max(B - 1, 1), z.quarter[c], LANES), bf16)
        + scratch(lambda c: (z.quarter[c], LANES), f32)
        + scratch(lambda c: (z.quarter[c], LANES), bf16)
        + scratch(lambda c: (max(A - 1, 1), z.piece[c], LANES), bf16)
        + scratch(lambda c: (z.n[c], z.cols[c]), f32) * 3
        + [pltpu.VMEM((k, z.small_rows, LANES), f32) for k in (S, B, A)]
        + [pltpu.SemaphoreType.DMA((9, S))] * 2
        + [pltpu.SemaphoreType.DMA((5, B))] * 2
        + [pltpu.SemaphoreType.DMA((5, A))] * 2
        + [pltpu.SemaphoreType.DMA((10,))],
        compiler_params=pltpu.CompilerParams(
            collective_id=0, has_side_effects=True, vmem_limit_bytes=40 * 1024 * 1024
        ),
        name="exchange",
    )(gq, go, gn, gb, wq, wo, wn, wb, fq, fo, fn, fb, sq, so, sn, sb)

    results = pl.pallas_call(
        functools.partial(finish_kernel, z),
        out_shape=[
            shape(whole[0], bf16), shape(whole[1], bf16),
            shape((1, wn.shape[1] * S), bf16), shape((z.b * S, z.heads), bf16),
        ]
        + [shape(ref.shape, f32) for ref in (fq, fo, fn, fb)] * 2
        + [shape((2, 4), f32), shape((1, 4), f32)],
        in_specs=[vmem] * 13,
        out_specs=[vmem] * 14,
        compiler_params=pltpu.CompilerParams(vmem_limit_bytes=40 * 1024 * 1024),
        name="finish",
    )(*outs, fq, fo, sq, so)
    results = list(results)
    for at in (2, 6, 10, 13):
        results[at] = results[at].reshape(-1)
    return tuple(results)


def solution(mesh):
    shards, replicas = mesh.shape["shard"], mesh.shape["replica"]
    every = ("replica", "shard")
    state = (P("shard", None), P("shard", None), P("shard"), P("shard", None))
    return jax.shard_map(
        functools.partial(on_device, shards, replicas),
        mesh=mesh,
        in_specs=(P(every, None, None), P(every, None, None), P(every, None), P(every, None, None)) + state * 3,
        out_specs=(P(), P(), P(), P()) + state * 2 + (P(), P()),
        check_vma=False,
    )
```

time: 188 us -> 45.9 us (0.24)
  waiting for transfers between devices: 95.6 us -> 0 us
  blocking collectives: 53.4 us -> 0 us
  Pallas kernels: 0 us -> 30.3 us
  between operations: 16.8 us -> 0.72 us
  other arithmetic: 16.4 us -> 0.58 us
  local copies, waits for them, and re-layouts: 4.81 us -> 13.7 us
    psum x1 -> x0, waiting for transfers between devices: 95 us -> none  [on_device(): lax.psum((gradients[0], gradients[1], gradients[2], gradients[3]), ('repl...]
    psum x2 -> x0, blocking collectives: 45.6 us -> none  [the longest x1 42.5 us: on_device(): lax.psum((gradients[0], gradients[1], gradients[2], gradients[3]), ('repl...]
    pallas_call x0 -> x2, Pallas kernels: none -> 30.3 us  [the longest x1 28.5 us: on_device(): pl.pallas_call(functools.partial(exchange_kernel, z), out_shape=[shape((z...]
    unnamed x50 -> x47, local copies, waits for them, and re-layouts: 4.21 us -> 13.7 us
    all_gather x4 -> x0, blocking collectives: 7.74 us -> none  [the longest x1 2.09 us: on_device(): lax.all_gather(shards[1], 'shard', axis=0, tiled=True)]
    div x1 -> x0, other arithmetic: 5.14 us -> none  [on_device(): trust_ratios = weight_sizes / (update_sizes + 1e-06)]
    sqrt x1 -> x0, other arithmetic: 5.13 us -> none  [on_device(): weight_sizes = jnp.sqrt(jnp.stack([couple[0] for couple in couples]))]
    reduce_sum x4 -> x0, other arithmetic: 5.08 us -> none  [on_device(): update_squares = [jnp.sum(result[2] * result[2]) for result in results]]
  transfers between devices with their start and end apart: 1 -> 0, of which waited for: 1 -> 0; matrix products, arithmetic and copies ran while one was open for 1% -> 0% of each run, Pallas kernels for 0% -> 0%
where the time goes in v1:
time: 45.9 us; the launch traced here: 45.3 us
  Pallas kernels  30.3 us (66%)
  local copies, waits for them, and re-layouts  13.7 us (30%)
  between operations  0.72 us (2%)
  other arithmetic  0.58 us (1%)
    pallas_call x1, Pallas kernels, on_device(): pl.pallas_call(functools.partial(exchange_kernel, z), out_shape=[shape((z...  28.5 us
    unnamed x47, local copies, waits for them, and re-layouts  13.7 us
    pallas_call x1, Pallas kernels, on_device(): pl.pallas_call(functools.partial(finish_kernel, z), out_shape=[shape(whol...  1.78 us

profile of v1, /device:TPU:0, one launch (start us, length us, event | category | flops | bytes accessed | tf_op | source)
XLA Modules:
  0.0 45.3 jit_solution(10264239029058023377)
XLA Ops:
  0.6 0.0 copy-start.16
  0.7 0.7 %copy-done.16 = f32[16,6]{0,1:T(8,128)S(1)} copy-done((f32[16,6]{0,1:T(8,128)S(1)}, f32[16,6]{0,1:T(8,128)}, u32[]{:S(2)}) %copy-start.16) | copy-done | bytes 408
  1.3 0.0 copy-start.17
  1.3 0.1 copy.31.wb
  1.4 0.6 %copy-done.17 = f32[16,6]{0,1:T(8,128)S(1)} copy-done((f32[16,6]{0,1:T(8,128)S(1)}, f32[16,6]{0,1:T(8,128)}, u32[]{:S(2)}) %copy-start.17) | copy-done | bytes 408
  2.0 0.1 copy.32.fb
  2.1 0.6 %copy-done.18 = f32[16,6]{0,1:T(8,128)S(1)} copy-done((f32[16,6]{0,1:T(8,128)S(1)}, f32[16,6]{0,1:T(8,128)}, u32[]{:S(2)}) %copy-start.18) | copy-done | bytes 408
  2.7 0.1 copy.33.sb
  2.8 0.6 %copy-done.19 = f32[1,32,6]{1,0,2:T(1,128)S(1)} copy-done((f32[1,32,6]{1,0,2:T(1,128)S(1)}, f32[1,32,6]{1,0,2:T(1,128)}, u32[]{:S(2)}) %copy-start.19) | copy-done | bytes 792
  3.4 0.1 copy.30.gb
  3.5 0.6 %copy-done.12 = f32[1,512]{1,0:T(1,128)S(1)} copy-done((f32[1,512]{1,0:T(1,128)S(1)}, f32[1,512]{1,0:T(1,128)}, u32[]{:S(2)}) %copy-start.12) | copy-done | bytes 2072
  4.1 0.0 copy-done.13
  4.1 0.0 copy-done.14
  4.1 0.0 copy-done.15
  4.1 1.0 %copy-done = f32[256,384]{1,0:T(8,128)S(1)} copy-done((f32[256,384]{1,0:T(8,128)S(1)}, f32[256,384]{1,0:T(8,128)}, u32[]{:S(2)}) %copy-start) | copy-done | bytes 393240
  5.1 1.0 %copy-done.2 = f32[192,512]{1,0:T(8,128)S(1)} copy-done((f32[192,512]{1,0:T(8,128)S(1)}, f32[192,512]{1,0:T(8,128)}, u32[]{:S(2)}) %copy-start.2) | copy-done | bytes 393240
  6.1 1.0 %copy-done.4 = f32[256,384]{1,0:T(8,128)S(1)} copy-done((f32[256,384]{1,0:T(8,128)S(1)}, f32[256,384]{1,0:T(8,128)}, u32[]{:S(2)}) %copy-start.4) | copy-done | bytes 393240
  7.1 1.0 %copy-done.6 = f32[192,512]{1,0:T(8,128)S(1)} copy-done((f32[192,512]{1,0:T(8,128)S(1)}, f32[192,512]{1,0:T(8,128)}, u32[]{:S(2)}) %copy-start.6) | copy-done | bytes 393240
  8.1 1.1 %copy-done.8 = f32[1,512,384]{2,1,0:T(8,128)S(1)} copy-done((f32[1,512,384]{2,1,0:T(8,128)S(1)}, f32[1,512,384]{2,1,0:T(8,128)}, u32[]{:S(2)}) %copy-start.8) | copy-done | bytes 786456
  9.2 1.1 %copy-done.9 = f32[1,384,512]{2,1,0:T(8,128)S(1)} copy-done((f32[1,384,512]{2,1,0:T(8,128)S(1)}, f32[1,384,512]{2,1,0:T(8,128)}, u32[]{:S(2)}) %copy-start.9) | copy-done | bytes 786456
  10.4 1.0 %copy-done.10 = f32[256,384]{1,0:T(8,128)S(1)} copy-done((f32[256,384]{1,0:T(8,128)S(1)}, f32[256,384]{1,0:T(8,128)}, u32[]{:S(2)}) %copy-start.10) | copy-done | bytes 393240
  11.4 1.0 %copy-done.11 = f32[192,512]{1,0:T(8,128)S(1)} copy-done((f32[192,512]{1,0:T(8,128)S(1)}, f32[192,512]{1,0:T(8,128)}, u32[]{:S(2)}) %copy-start.11) | copy-done | bytes 393240
  12.4 28.5 %exchange.1 = (bf16[768,128]{1,0:T(8,128)(2,1)S(1)}, bf16[768,128]{1,0:T(8,128)(2,1)S(1)}, bf16[512,384]{1,0:T(8,128)(2,1)S(1)}, bf16[384,512]{1,0:T(8,128)(2,1)...) custom-call(f32[1,512,384]{2,1,0:T(8,128)S(1)} %copy-done.8, ...), custom_call_target="tpu_custom_call" | custom-call | tf_op jit(solution)/shard_map/exchange/pallas_call | solution.py:370
  40.9 0.0 copy-done.1
  40.9 0.0 copy-done.3
  40.9 0.0 copy-done.5
  40.9 0.0 copy-done.7
  40.9 1.8 %finish.1 = (bf16[512,384]{1,0:T(8,128)(2,1)}, bf16[384,512]{1,0:T(8,128)(2,1)}, bf16[1,512]{1,0:T(2,128)(2,1)S(1)}, bf16[32,6]{1,0:T(8,128)(2,1)S(1)}, f32[256,...) custom-call(bf16[768,128]{1,0:T(8,128)(2,1)S(1)} %get-tuple-element., ...), custom_call_target="tpu_custom_call" | custom-call | tf_op jit(solution)/shard_map/finish/pallas_call | solution.py:397
  42.7 0.6 %reduce = bf16[512]{0:T(512)(128)(2,1)} reduce(bf16[1,512]{1,0:T(2,128)(2,1)S(1)} %get-tuple-element.48, bf16[]{:T(256)} %constant.4), dimensions={0}, to_apply=%get-tuple-element.48.reduce_sub_computation | reduce | bytes 2050 | tf_op jit(solution)/shard_map/finish/pallas_call | solution.py:397
  43.3 0.7 %copy.34 = bf16[32,6]{0,1:T(8,128)(2,1)} copy(bf16[32,6]{1,0:T(8,128)(2,1)S(1)} %get-tuple-element.63) | data formatting | bytes 768
  43.9 0.7 %copy.35 = f32[16,6]{0,1:T(8,128)} copy(f32[16,6]{1,0:T(8,128)S(1)} %get-tuple-element.67) | data formatting | bytes 768
  44.6 0.7 %copy.36 = f32[16,6]{0,1:T(8,128)} copy(f32[16,6]{1,0:T(8,128)S(1)} %get-tuple-element.71) | data formatting | bytes 768
  (18 shorter events, 0.0 us)
Async XLA Ops:
  0.6 0.7 %copy-start.16 = (f32[16,6]{0,1:T(8,128)S(1)}, f32[16,6]{0,1:T(8,128)}, u32[]{:S(2)}) copy-start(f32[16,6]{0,1:T(8,128)} %param.23) | copy-start | bytes 1156
  1.3 0.7 %copy-start.17 = (f32[16,6]{0,1:T(8,128)S(1)}, f32[16,6]{0,1:T(8,128)}, u32[]{:S(2)}) copy-start(f32[16,6]{0,1:T(8,128)} %param.27) | copy-start | bytes 1156
  2.0 0.7 %copy-start.18 = (f32[16,6]{0,1:T(8,128)S(1)}, f32[16,6]{0,1:T(8,128)}, u32[]{:S(2)}) copy-start(f32[16,6]{0,1:T(8,128)} %param.31) | copy-start | bytes 1156
  2.7 0.7 %copy-start.19 = (f32[1,32,6]{1,0,2:T(1,128)S(1)}, f32[1,32,6]{1,0,2:T(1,128)}, u32[]{:S(2)}) copy-start(f32[1,32,6]{1,0,2:T(1,128)} %param.19) | copy-start | bytes 2308
  3.4 0.7 %copy-start.12 = (f32[1,512]{1,0:T(1,128)S(1)}, f32[1,512]{1,0:T(1,128)}, u32[]{:S(2)}) copy-start(f32[1,512]{1,0:T(1,128)} %gn.1) | copy-start | bytes 6148
  3.4 0.7 %copy-start.13 = (f32[256]{0:T(256)S(1)}, f32[256]{0:T(256)}, u32[]{:S(2)}) copy-start(f32[256]{0:T(256)} %param.22) | copy-start | bytes 3076
  3.4 0.7 %copy-start.14 = (f32[256]{0:T(256)S(1)}, f32[256]{0:T(256)}, u32[]{:S(2)}) copy-start(f32[256]{0:T(256)} %param.26) | copy-start | bytes 3076
  3.4 0.7 %copy-start.15 = (f32[256]{0:T(256)S(1)}, f32[256]{0:T(256)}, u32[]{:S(2)}) copy-start(f32[256]{0:T(256)} %param.30) | copy-start | bytes 3076
  4.1 1.0 %copy-start = (f32[256,384]{1,0:T(8,128)S(1)}, f32[256,384]{1,0:T(8,128)}, u32[]{:S(2)}) copy-start(f32[256,384]{1,0:T(8,128)} %fq.3) | copy-start | bytes 1179652
  5.1 1.0 %copy-start.2 = (f32[192,512]{1,0:T(8,128)S(1)}, f32[192,512]{1,0:T(8,128)}, u32[]{:S(2)}) copy-start(f32[192,512]{1,0:T(8,128)} %fo.3) | copy-start | bytes 1179652
  6.1 1.0 %copy-start.4 = (f32[256,384]{1,0:T(8,128)S(1)}, f32[256,384]{1,0:T(8,128)}, u32[]{:S(2)}) copy-start(f32[256,384]{1,0:T(8,128)} %sq.3) | copy-start | bytes 1179652
  7.1 1.0 %copy-start.6 = (f32[192,512]{1,0:T(8,128)S(1)}, f32[192,512]{1,0:T(8,128)}, u32[]{:S(2)}) copy-start(f32[192,512]{1,0:T(8,128)} %so.3) | copy-start | bytes 1179652
  8.1 1.1 %copy-start.8 = (f32[1,512,384]{2,1,0:T(8,128)S(1)}, f32[1,512,384]{2,1,0:T(8,128)}, u32[]{:S(2)}) copy-start(f32[1,512,384]{2,1,0:T(8,128)} %gq.1) | copy-start | bytes 2359300
  9.2 1.1 %copy-start.9 = (f32[1,384,512]{2,1,0:T(8,128)S(1)}, f32[1,384,512]{2,1,0:T(8,128)}, u32[]{:S(2)}) copy-start(f32[1,384,512]{2,1,0:T(8,128)} %go.1) | copy-start | bytes 2359300
  10.4 1.0 %copy-start.10 = (f32[256,384]{1,0:T(8,128)S(1)}, f32[256,384]{1,0:T(8,128)}, u32[]{:S(2)}) copy-start(f32[256,384]{1,0:T(8,128)} %wq.1) | copy-start | bytes 1179652
  11.4 1.0 %copy-start.11 = (f32[192,512]{1,0:T(8,128)S(1)}, f32[192,512]{1,0:T(8,128)}, u32[]{:S(2)}) copy-start(f32[192,512]{1,0:T(8,128)} %wo.1) | copy-start | bytes 1179652
  12.4 28.5 %copy-start.1 = (f32[256,384]{1,0:T(8,128)S(1)}, f32[256,384]{1,0:T(8,128)}, u32[]{:S(2)}) copy-start(f32[256,384]{1,0:T(8,128)} %fq.3) | copy-start | bytes 1179652
  12.4 28.5 %copy-start.3 = (f32[192,512]{1,0:T(8,128)S(1)}, f32[192,512]{1,0:T(8,128)}, u32[]{:S(2)}) copy-start(f32[192,512]{1,0:T(8,128)} %fo.3) | copy-start | bytes 1179652
  12.4 28.5 %copy-start.5 = (f32[256,384]{1,0:T(8,128)S(1)}, f32[256,384]{1,0:T(8,128)}, u32[]{:S(2)}) copy-start(f32[256,384]{1,0:T(8,128)} %sq.3) | copy-start | bytes 1179652
  12.4 28.5 %copy-start.7 = (f32[192,512]{1,0:T(8,128)S(1)}, f32[192,512]{1,0:T(8,128)}, u32[]{:S(2)}) copy-start(f32[192,512]{1,0:T(8,128)} %so.3) | copy-start | bytes 1179652

commit v2 on v1

--- a/solution.py
+++ b/solution.py
@@ -31,11 +31,12 @@
         self.L = min(LANES, norm[0])
         self.q = norm[0] // self.L
         self.norm_rows = up(self.q * shards, 8)
-        self.b, self.heads = bias
-        self.small_rows = up(self.norm_rows + self.b * shards, 8)
+        self.heads, self.b = bias
+        self.hp = up(self.heads, 8)
+        self.small_rows = self.norm_rows + self.hp
         self.state_norm = up(3 * self.q, 8)
-        self.bp = up(self.b, 8)
-        self.state_rows = self.state_norm + 3 * self.bp
+        self.state_rows = self.state_norm + 3 * self.hp
+        self.sum_rows = up(2 * (self.B + 1), 8)
 
 
 def step_math(summed, moment, second):
@@ -46,12 +47,13 @@
 
 def exchange_kernel(
     z,
-    gq, go, gn, gb, wq, wo, wn, wb, fq, fo, fn, fb, sq, so, sn, sb,
+    gq, go, gn_h, gb_h, wq, wo, wn_h, wb_h, fq, fo, fn_h, fb_h, sq, so, sn_h, sb_h,
     fin_q, fin_o, u_q, u_o, full_q, full_o, small_out, state, sums,
     core_q, core_o, acc_q, acc_o, send_q, send_o, plane_q, plane_o,
     quarter_q, quarter_o, zsend_q, zsend_o, zin_q, zin_o,
     wv_q, wv_o, fv_q, fv_o, sv_q, sv_o, small_core, small_plane, small_z,
-    shard_send, shard_recv, plane_send, plane_recv, z_send, z_recv, local,
+    gn, gb, wn, wb, fn, fb, sn, sb,
+    shard_send, shard_recv, plane_send, plane_recv, z_send, z_recv, local, packing,
 ):
     S, B, A = z.S, z.B, z.A
     s = lax.axis_index("shard")
@@ -113,6 +115,14 @@
         copy.start()
         own.append(copy)
 
+    tiny = []
+    for i, (src, dst) in enumerate((
+        (gn_h, gn), (gb_h, gb), (wn_h, wn), (wb_h, wb), (fn_h, fn), (fb_h, fb), (sn_h, sn), (sb_h, sb),
+    )):
+        copy = pltpu.make_async_copy(src, dst, local.at[2 + i])
+        copy.start()
+        tiny.append(copy)
+
     barrier = pltpu.get_barrier_semaphore()
     for d in range(1, S):
         pl.semaphore_signal(barrier, inc=1, device_id=(r, shard_peer(d)), device_id_type=MESH)
@@ -121,32 +131,42 @@
     for d in range(1, A):
         pl.semaphore_signal(barrier, inc=1, device_id=z_peer(d), device_id_type=MESH)
 
+    pl.semaphore_wait(barrier, S + B + A - 3)
+
+    core_in = [
+        to_shard(c, lambda peer, c=c: grads[c].at[0, rows(peer, z.n[c], 8), :], cores[c].at[s])
+        for c in range(2)
+    ]
+
+    for copy in tiny:
+        copy.wait()
     small_core[s] = jnp.zeros((z.small_rows, LANES), jnp.float32)
     for i in range(z.q * S):
         small_core[s, i : i + 1, : z.L] = gn[:, i * z.L : (i + 1) * z.L]
-    small_core[s, z.norm_rows : z.norm_rows + z.b * S, : z.heads] = gb[0]
+    for h in range(z.heads):
+        small_core[s, z.norm_rows + h : z.norm_rows + h + 1, : z.b * S] = gb[h]
     state[s] = jnp.zeros((z.state_rows, LANES), jnp.float32)
     for t, ref in enumerate((wn, fn, sn)):
         for i in range(z.q):
             row = t * z.q + i
             state[s, row : row + 1, : z.L] = ref[:, i * z.L : (i + 1) * z.L]
     for t, ref in enumerate((wb, fb, sb)):
-        row = z.state_norm + t * z.bp
-        state[s, row : row + z.b, : z.heads] = ref[...]
-
-    pl.semaphore_wait(barrier, S + B + A - 3)
-
-    core_in = [
-        to_shard(c, lambda peer, c=c: grads[c].at[0, rows(peer, z.n[c], 8), :], cores[c].at[s])
-        for c in range(2)
-    ]
+        row = z.state_norm + t * z.hp
+        state[s, row : row + z.heads, : z.b] = ref[...]
     small_in = to_shard(2, lambda peer: small_core.at[s], small_core.at[s])
+
     held = []
     for c in range(2):
+        n = z.n[c]
         for t, (src, dst) in enumerate(((weights[c], wvs[c]), (firsts[c], fvs[c]), (seconds[c], svs[c]))):
-            copy = pltpu.make_async_copy(src, dst, local.at[2 + 3 * c + t])
-            copy.start()
-            held.append(copy)
+            for j in range(z.blocks[c]):
+                copy = pltpu.make_async_copy(
+                    src.at[:, j * LANES : (j + 1) * LANES], dst.at[j * n : (j + 1) * n, :], packing.at[3 * c + t, j]
+                )
+                copy.start()
+                held.append(copy)
+            if z.used[c] < z.total[c]:
+                dst[z.used[c] :, :] = jnp.zeros((z.total[c] - z.used[c], LANES), jnp.float32)
 
     plane_in = []
     for c in range(2):
@@ -180,7 +200,7 @@
     late = []
     for c in range(2):
         late += to_shard(3 + c, lambda peer, c=c: weights[c], fulls[c].at[rows(s, z.n[c], 8), :])
-        copy = pltpu.make_async_copy(weights[c], fulls[c].at[rows(s, z.n[c], 8), :], local.at[8 + c])
+        copy = pltpu.make_async_copy(weights[c], fulls[c].at[rows(s, z.n[c], 8), :], local.at[10 + c])
         copy.start()
         held.append(copy)
     late += to_shard(5, lambda peer: state.at[s], state.at[s])
@@ -226,36 +246,37 @@
         back_plane.append(
             to_plane(3 + c, lambda peer, c=c, mine=mine: fins[c].at[mine, :], lambda d, c=c, mine=mine: fins[c].at[mine, :])
         )
+    for copy in held:
+        copy.wait()
+    sums[s] = jnp.zeros((z.sum_rows, LANES), jnp.float32)
+    for c in range(2):
+        weight = wvs[c][...]
+        sums[s, c * (B + 1) : c * (B + 1) + 1, :] = jnp.sum(weight * weight, axis=0, keepdims=True)
+
+    def updates(c, d):
+        index = lax.rem(b + B - d, B)
+        mine = rows(index, z.quarter[c], 16)
+        summed = fins[c][mine, :].astype(jnp.float32)
+        _, _, update = step_math(summed, fvs[c][mine, :], svs[c][mine, :])
+        update = update + DECAY * wvs[c][mine, :]
+        sums[s, pl.ds(c * (B + 1) + 1 + index, 1), :] = jnp.sum(update * update, axis=0, keepdims=True)
+        us[c][s, mine, :] = update.astype(jnp.bfloat16)
+        return to_shard(
+            6 + c * B + d, lambda peer: us[c].at[s, mine, :], us[c].at[s, mine, :]
+        )
+
+    for c in range(2):
+        late += updates(c, 0)
     arrived(small_in)
     small = small_z[0]
     for k in range(1, A):
         small = small + small_z[k]
     small_out[...] = small
-    for copy in held:
-        copy.wait()
-    sums[s] = jnp.zeros((8, LANES), jnp.float32)
-    for c in range(2):
-        squares = jnp.zeros((1, LANES), jnp.float32)
-        for j in range(z.blocks[c]):
-            weight = wvs[c][:, j * LANES : (j + 1) * LANES]
-            squares = squares + jnp.sum(weight * weight, axis=0, keepdims=True)
-        sums[s, 2 * c : 2 * c + 1, :] = squares
-
-    for c in range(2):
-        arrived(back_plane[c])
-        n = z.n[c]
-        mine = rows(s, n, 16)
-        squares = jnp.zeros((1, LANES), jnp.float32)
-        for j in range(z.blocks[c]):
-            lanes = slice(j * LANES, (j + 1) * LANES)
-            summed = fins[c][j * n : (j + 1) * n, :].astype(jnp.float32)
-            _, _, update = step_math(summed, fvs[c][:, lanes], svs[c][:, lanes])
-            update = update + DECAY * wvs[c][:, lanes]
-            squares = squares + jnp.sum(update * update, axis=0, keepdims=True)
-            us[c][mine, lanes] = update.astype(jnp.bfloat16)
-        sums[s, 2 * c + 1 : 2 * c + 2, :] = squares
-        late += to_shard(6 + c, lambda peer, c=c, mine=mine: us[c].at[mine, :], us[c].at[mine, :])
-    late += to_shard(8, lambda peer: sums.at[s], sums.at[s])
+    for c in range(2):
+        for d in range(1, B):
+            back_plane[c][d - 1].wait_recv()
+            late += updates(c, d)
+    late += to_shard(6 + 2 * B, lambda peer: sums.at[s], sums.at[s])
     arrived(late)
     for copy in started:
         copy.wait_send()
@@ -273,18 +294,21 @@
     for k in range(1, S):
         totals = totals + sums[k]
 
-    def whole(row):
-        return jnp.sum(totals[row : row + 1, :], axis=1, keepdims=True)
-
-    squares = [(whole(0), whole(1)), (whole(2), whole(3))]
+    def whole(row, count):
+        value = totals[row : row + 1, :]
+        for i in range(1, count):
+            value = value + totals[row + i : row + i + 1, :]
+        return jnp.sum(value, axis=1, keepdims=True)
+
+    squares = [(whole(c * (z.B + 1), 1), whole(c * (z.B + 1) + 1, z.B)) for c in range(2)]
 
     def norm_of(k):
         rows = [state[k, t * z.q : (t + 1) * z.q, :L] for t in range(3)]
         return small[pl.ds(k * z.q, z.q), :L], rows
 
     def bias_of(k):
-        rows = [state[k, z.state_norm + t * z.bp : z.state_norm + t * z.bp + z.b, :h] for t in range(3)]
-        return small[pl.ds(z.norm_rows + k * z.b, z.b), :h], rows
+        rows = [state[k, z.state_norm + t * z.hp : z.state_norm + t * z.hp + h, : z.b] for t in range(3)]
+        return small[z.norm_rows : z.norm_rows + h, k * z.b : (k + 1) * z.b], rows
 
     def total(value):
         return jnp.sum(jnp.sum(value, axis=0, keepdims=True), axis=1, keepdims=True)
@@ -323,16 +347,20 @@
         value = (weight - 0.01 * ratios[2] * update).astype(jnp.bfloat16)
         for i in range(z.q):
             at = (k * z.q + i) * L
-            new_n[:, at : at + L] = value[i : i + 1, :]
+            new_n[at : at + L] = value[i]
         weight, update = pairs[1][k]
-        new_b[k * z.b : (k + 1) * z.b, :] = (weight - 0.01 * ratios[3] * update).astype(jnp.bfloat16)
+        new_b[:, k * z.b : (k + 1) * z.b] = (weight - 0.01 * ratios[3] * update).astype(jnp.bfloat16)
     summed, (_, moment, second) = norm_of(s)
     moment_next, second_next, _ = step_math(summed, moment, second)
     for i in range(z.q):
         fn_next[:, i * L : (i + 1) * L] = moment_next[i : i + 1, :]
         sn_next[:, i * L : (i + 1) * L] = second_next[i : i + 1, :]
-    summed, (_, moment, second) = bias_of(s)
-    moment_next, second_next, _ = step_math(summed, moment, second)
+    moment_next = second_next = jnp.zeros((h, z.b), jnp.float32)
+    for k in range(S):
+        summed, (_, moment, second) = bias_of(k)
+        moment_value, second_value, _ = step_math(summed, moment, second)
+        moment_next = jnp.where(s == k, moment_value, moment_next)
+        second_next = jnp.where(s == k, second_value, second_next)
     fb_next[...] = moment_next
     sb_next[...] = second_next
 
@@ -347,7 +375,10 @@
             moment_value, second_value, _ = step_math(summed, first[:, lanes], second[:, lanes])
             first_next[:, lanes] = moment_value
             second_next[:, lanes] = second_value
-        new[...] = (full[...] - 0.01 * ratios[c] * u[...].astype(jnp.float32)).astype(jnp.bfloat16)
+            for k in range(S):
+                own = slice(k * n, (k + 1) * n)
+                update = u[k, j * n : (j + 1) * n, :].astype(jnp.float32)
+                new[own, lanes] = (full[own, lanes] - 0.01 * ratios[c] * update).astype(jnp.bfloat16)
 
 
 def on_device(
@@ -355,6 +386,8 @@
     gq, go, gn, gb, wq, wo, wn, wb, fq, fo, fn, fb, sq, so, sn, sb,
 ):
     f32, bf16 = jnp.float32, jnp.bfloat16
+    wb, fb, sb = (value.T for value in (wb, fb, sb))
+    gb = jnp.transpose(gb, (2, 0, 1))
     z = Sizes(shards, replicas, wq.shape, wo.shape, wn.shape, wb.shape)
     S, B, A = z.S, z.B, z.A
     wn, fn, sn = (value.reshape(1, -1) for value in (wn, fn, sn))
@@ -370,10 +403,10 @@
     outs = pl.pallas_call(
         functools.partial(exchange_kernel, z),
         out_shape=[shape((z.total[c], LANES), bf16) for c in both]
-        + [shape(whole[c], bf16) for c in both]
+        + [shape((S, z.total[c], LANES), bf16) for c in both]
         + [shape(whole[c], f32) for c in both]
-        + [shape((z.small_rows, LANES), f32), shape((S, z.state_rows, LANES), f32), shape((S, 8, LANES), f32)],
-        in_specs=[any_spec, any_spec, vmem, vmem] + [any_spec, any_spec, vmem, vmem] * 3,
+        + [shape((z.small_rows, LANES), f32), shape((S, z.state_rows, LANES), f32), shape((S, z.sum_rows, LANES), f32)],
+        in_specs=[pl.BlockSpec(memory_space=pltpu.HBM)] * 16,
         out_specs=[vmem] * 4 + [any_spec] * 2 + [vmem] * 3,
         scratch_shapes=scratch(lambda c: (S, z.n[c], z.cols[c]), f32)
         + scratch(lambda c: (z.total[c], LANES), f32)
@@ -382,14 +415,15 @@
         + scratch(lambda c: (z.quarter[c], LANES), f32)
         + scratch(lambda c: (z.quarter[c], LANES), bf16)
         + scratch(lambda c: (max(A - 1, 1), z.piece[c], LANES), bf16)
-        + scratch(lambda c: (z.n[c], z.cols[c]), f32) * 3
+        + scratch(lambda c: (z.total[c], LANES), f32) * 3
         + [pltpu.VMEM((k, z.small_rows, LANES), f32) for k in (S, B, A)]
-        + [pltpu.SemaphoreType.DMA((9, S))] * 2
+        + [pltpu.VMEM(value.shape, f32) for value in (gn, gb, wn, wb, fn, fb, sn, sb)]
+        + [pltpu.SemaphoreType.DMA((7 + 2 * B, S))] * 2
         + [pltpu.SemaphoreType.DMA((5, B))] * 2
         + [pltpu.SemaphoreType.DMA((5, A))] * 2
-        + [pltpu.SemaphoreType.DMA((10,))],
+        + [pltpu.SemaphoreType.DMA((12,)), pltpu.SemaphoreType.DMA((6, max(z.blocks)))],
         compiler_params=pltpu.CompilerParams(
-            collective_id=0, has_side_effects=True, vmem_limit_bytes=40 * 1024 * 1024
+            collective_id=0, has_side_effects=True, vmem_limit_bytes=60 * 1024 * 1024
         ),
         name="exchange",
     )(gq, go, gn, gb, wq, wo, wn, wb, fq, fo, fn, fb, sq, so, sn, sb)
@@ -398,7 +432,7 @@
         functools.partial(finish_kernel, z),
         out_shape=[
             shape(whole[0], bf16), shape(whole[1], bf16),
-            shape((1, wn.shape[1] * S), bf16), shape((z.b * S, z.heads), bf16),
+            shape((wn.shape[1] * S,), bf16), shape((z.heads, z.b * S), bf16),
         ]
         + [shape(ref.shape, f32) for ref in (fq, fo, fn, fb)] * 2
         + [shape((2, 4), f32), shape((1, 4), f32)],
@@ -408,8 +442,10 @@
         name="finish",
     )(*outs, fq, fo, sq, so)
     results = list(results)
-    for at in (2, 6, 10, 13):
+    for at in (6, 10, 13):
         results[at] = results[at].reshape(-1)
+    for at in (3, 7, 11):
+        results[at] = results[at].T
     return tuple(results)
 
 

time: 45.9 us -> 48.3 us (1.052)
  Pallas kernels: 30.3 us -> 38.8 us
  local copies, waits for them, and re-layouts: 13.7 us -> 8.25 us
  other arithmetic: 0.58 us -> 0 us
    pallas_call x1, Pallas kernels: 28.5 us -> 36.9 us  [on_device(): pl.pallas_call(functools.partial(exchange_kernel, z), out_shape=[shape((z...]
    unnamed x47 -> x26, local copies, waits for them, and re-layouts: 13.7 us -> 8.25 us
    pallas_call x1 -> x0, other arithmetic: 0.58 us -> none  [on_device(): pl.pallas_call(functools.partial(finish_kernel, z), out_shape=[shape(whol...]
where the time goes in v2:
time: 48.3 us; the launch traced here: 47.8 us
  Pallas kernels  38.8 us (80%)
  local copies, waits for them, and re-layouts  8.25 us (17%)
  between operations  0.74 us (2%)
    pallas_call x1, Pallas kernels, on_device(): pl.pallas_call(functools.partial(exchange_kernel, z), out_shape=[shape((z...  36.9 us
    unnamed x26, local copies, waits for them, and re-layouts  8.25 us
    pallas_call x1, Pallas kernels, on_device(): pl.pallas_call(functools.partial(finish_kernel, z), out_shape=[shape(whol...  1.9 us

profile of v2, /device:TPU:0, one launch (start us, length us, event | category | flops | bytes accessed | tf_op | source)
XLA Modules:
  0.0 47.8 jit_solution(2977640439698846567)
XLA Ops:
  0.7 0.0 copy-start
  0.7 0.0 copy-start.1
  0.7 0.0 copy-start.2
  0.7 0.0 copy-start.3
  0.7 36.9 %exchange.1 = (bf16[768,128]{1,0:T(8,128)(2,1)}, bf16[768,128]{1,0:T(8,128)(2,1)}, bf16[2,768,128]{2,1,0:T(8,128)(2,1)}, bf16[2,768,128]{2,1,0:T(8,128)(2,1)}, f...) custom-call(f32[1,512,384]{2,1,0:T(8,128)} %gq.1, ...), custom_call_target="tpu_custom_call" | custom-call | tf_op jit(solution)/shard_map/exchange/pallas_call | solution.py:403
  37.6 0.0 copy-start.11
  37.6 0.0 copy-done
  37.6 0.0 copy-done.1
  37.6 0.0 copy-done.2
  37.6 0.0 copy-done.3
  37.6 0.7 %copy-done.11 = f32[2,16,128]{2,1,0:T(8,128)S(1)} copy-done((f32[2,16,128]{2,1,0:T(8,128)S(1)}, f32[2,16,128]{2,1,0:T(8,128)}, u32[]{:S(2)}) %copy-start.11) | copy-done | bytes 16408
  38.3 0.0 copy-start.4
  38.3 1.1 %copy-done.4 = f32[512,384]{1,0:T(8,128)S(1)} copy-done((f32[512,384]{1,0:T(8,128)S(1)}, f32[512,384]{1,0:T(8,128)}, u32[]{:S(2)}) %copy-start.4) | copy-done | bytes 786456
  39.4 0.0 copy-start.5
  39.4 1.1 %copy-done.5 = f32[384,512]{1,0:T(8,128)S(1)} copy-done((f32[384,512]{1,0:T(8,128)S(1)}, f32[384,512]{1,0:T(8,128)}, u32[]{:S(2)}) %copy-start.5) | copy-done | bytes 786456
  40.6 0.0 copy-start.6
  40.6 1.0 %copy-done.6 = bf16[2,768,128]{2,1,0:T(8,128)(2,1)S(1)} copy-done((bf16[2,768,128]{2,1,0:T(8,128)(2,1)S(1)}, bf16[2,768,128]{2,1,0:T(8,128)(2,1)}, u32[]{:S(2)}) %copy-start.6) | copy-done | bytes 393240
  41.6 0.0 copy-start.7
  41.6 1.0 %copy-done.7 = bf16[2,768,128]{2,1,0:T(8,128)(2,1)S(1)} copy-done((bf16[2,768,128]{2,1,0:T(8,128)(2,1)S(1)}, bf16[2,768,128]{2,1,0:T(8,128)(2,1)}, u32[]{:S(2)}) %copy-start.7) | copy-done | bytes 393240
  42.6 0.0 copy-start.8
  42.6 0.9 %copy-done.8 = bf16[768,128]{1,0:T(8,128)(2,1)S(1)} copy-done((bf16[768,128]{1,0:T(8,128)(2,1)S(1)}, bf16[768,128]{1,0:T(8,128)(2,1)}, u32[]{:S(2)}) %copy-start.8) | copy-done | bytes 196632
  43.5 0.0 copy-start.9
  43.5 0.9 %copy-done.9 = bf16[768,128]{1,0:T(8,128)(2,1)S(1)} copy-done((bf16[768,128]{1,0:T(8,128)(2,1)S(1)}, bf16[768,128]{1,0:T(8,128)(2,1)}, u32[]{:S(2)}) %copy-start.9) | copy-done | bytes 196632
  44.4 0.0 copy-start.10
  44.4 0.8 %copy-done.10 = f32[2,32,128]{2,1,0:T(8,128)S(1)} copy-done((f32[2,32,128]{2,1,0:T(8,128)S(1)}, f32[2,32,128]{2,1,0:T(8,128)}, u32[]{:S(2)}) %copy-start.10) | copy-done | bytes 32792
  45.2 0.0 copy-start.12
  45.2 0.7 %copy-done.12 = f32[16,128]{1,0:T(8,128)S(1)} copy-done((f32[16,128]{1,0:T(8,128)S(1)}, f32[16,128]{1,0:T(8,128)}, u32[]{:S(2)}) %copy-start.12) | copy-done | bytes 8216
  45.9 1.9 %finish.1 = (bf16[512,384]{1,0:T(8,128)(2,1)}, bf16[384,512]{1,0:T(8,128)(2,1)}, bf16[512]{0:T(512)(128)(2,1)}, bf16[6,32]{1,0:T(8,128)(2,1)}, f32[256,384]{1,0:...) custom-call(bf16[768,128]{1,0:T(8,128)(2,1)S(1)} %copy-done.8, ...), custom_call_target="tpu_custom_call" | custom-call | tf_op jit(solution)/shard_map/finish/pallas_call | solution.py:431
Async XLA Ops:
  0.7 36.9 %copy-start = (f32[256,384]{1,0:T(8,128)S(1)}, f32[256,384]{1,0:T(8,128)}, u32[]{:S(2)}) copy-start(f32[256,384]{1,0:T(8,128)} %fq.3) | copy-start | bytes 1179652
  0.7 36.9 %copy-start.1 = (f32[192,512]{1,0:T(8,128)S(1)}, f32[192,512]{1,0:T(8,128)}, u32[]{:S(2)}) copy-start(f32[192,512]{1,0:T(8,128)} %fo.3) | copy-start | bytes 1179652
  0.7 36.9 %copy-start.2 = (f32[256,384]{1,0:T(8,128)S(1)}, f32[256,384]{1,0:T(8,128)}, u32[]{:S(2)}) copy-start(f32[256,384]{1,0:T(8,128)} %sq.3) | copy-start | bytes 1179652
  0.7 36.9 %copy-start.3 = (f32[192,512]{1,0:T(8,128)S(1)}, f32[192,512]{1,0:T(8,128)}, u32[]{:S(2)}) copy-start(f32[192,512]{1,0:T(8,128)} %so.3) | copy-start | bytes 1179652
  37.6 0.7 %copy-start.11 = (f32[2,16,128]{2,1,0:T(8,128)S(1)}, f32[2,16,128]{2,1,0:T(8,128)}, u32[]{:S(2)}) copy-start(f32[2,16,128]{2,1,0:T(8,128)} %get-tuple-element.45.sums) | copy-start | bytes 49156
  38.3 1.1 %copy-start.4 = (f32[512,384]{1,0:T(8,128)S(1)}, f32[512,384]{1,0:T(8,128)}, u32[]{:S(2)}) copy-start(f32[512,384]{1,0:T(8,128)} %get-tuple-element.41.full_q) | copy-start | bytes 2359300
  39.4 1.1 %copy-start.5 = (f32[384,512]{1,0:T(8,128)S(1)}, f32[384,512]{1,0:T(8,128)}, u32[]{:S(2)}) copy-start(f32[384,512]{1,0:T(8,128)} %get-tuple-element.42.full_o) | copy-start | bytes 2359300
  40.6 1.0 %copy-start.6 = (bf16[2,768,128]{2,1,0:T(8,128)(2,1)S(1)}, bf16[2,768,128]{2,1,0:T(8,128)(2,1)}, u32[]{:S(2)}) copy-start(bf16[2,768,128]{2,1,0:T(8,128)(2,1)} %get-tuple-element.39.u_q) | copy-start | bytes 1179652
  41.6 1.0 %copy-start.7 = (bf16[2,768,128]{2,1,0:T(8,128)(2,1)S(1)}, bf16[2,768,128]{2,1,0:T(8,128)(2,1)}, u32[]{:S(2)}) copy-start(bf16[2,768,128]{2,1,0:T(8,128)(2,1)} %get-tuple-element.40.u_o) | copy-start | bytes 1179652
  42.6 0.9 %copy-start.8 = (bf16[768,128]{1,0:T(8,128)(2,1)S(1)}, bf16[768,128]{1,0:T(8,128)(2,1)}, u32[]{:S(2)}) copy-start(bf16[768,128]{1,0:T(8,128)(2,1)} %get-tuple-element.37.fin_q) | copy-start | bytes 589828
  43.5 0.9 %copy-start.9 = (bf16[768,128]{1,0:T(8,128)(2,1)S(1)}, bf16[768,128]{1,0:T(8,128)(2,1)}, u32[]{:S(2)}) copy-start(bf16[768,128]{1,0:T(8,128)(2,1)} %get-tuple-element.38.fin_o) | copy-start | bytes 589828
  44.4 0.8 %copy-start.10 = (f32[2,32,128]{2,1,0:T(8,128)S(1)}, f32[2,32,128]{2,1,0:T(8,128)}, u32[]{:S(2)}) copy-start(f32[2,32,128]{2,1,0:T(8,128)} %get-tuple-element.44.state) | copy-start | bytes 98308
  45.2 0.7 %copy-start.12 = (f32[16,128]{1,0:T(8,128)S(1)}, f32[16,128]{1,0:T(8,128)}, u32[]{:S(2)}) copy-start(f32[16,128]{1,0:T(8,128)} %get-tuple-element.43.small) | copy-start | bytes 24580

commit v3 on v2

--- a/solution.py
+++ b/solution.py
@@ -51,7 +51,7 @@
     fin_q, fin_o, u_q, u_o, full_q, full_o, small_out, state, sums,
     core_q, core_o, acc_q, acc_o, send_q, send_o, plane_q, plane_o,
     quarter_q, quarter_o, zsend_q, zsend_o, zin_q, zin_o,
-    wv_q, wv_o, fv_q, fv_o, sv_q, sv_o, small_core, small_plane, small_z,
+    fv_q, fv_o, sv_q, sv_o, small_core, small_plane, small_z,
     gn, gb, wn, wb, fn, fb, sn, sb,
     shard_send, shard_recv, plane_send, plane_recv, z_send, z_recv, local, packing,
 ):
@@ -63,7 +63,7 @@
     fins, us, fulls = (fin_q, fin_o), (u_q, u_o), (full_q, full_o)
     cores, accs, sends, planes = (core_q, core_o), (acc_q, acc_o), (send_q, send_o), (plane_q, plane_o)
     quarters, zsends, zins = (quarter_q, quarter_o), (zsend_q, zsend_o), (zin_q, zin_o)
-    wvs, fvs, svs = (wv_q, wv_o), (fv_q, fv_o), (sv_q, sv_o)
+    fvs, svs = (fv_q, fv_o), (sv_q, sv_o)
     started = []
 
     def shard_peer(d):
@@ -155,16 +155,16 @@
         state[s, row : row + z.heads, : z.b] = ref[...]
     small_in = to_shard(2, lambda peer: small_core.at[s], small_core.at[s])
 
-    held = []
+    held = ([], [])
     for c in range(2):
         n = z.n[c]
-        for t, (src, dst) in enumerate(((weights[c], wvs[c]), (firsts[c], fvs[c]), (seconds[c], svs[c]))):
+        for t, (src, dst) in enumerate(((weights[c], fulls[c].at[s]), (firsts[c], fvs[c]), (seconds[c], svs[c]))):
             for j in range(z.blocks[c]):
                 copy = pltpu.make_async_copy(
                     src.at[:, j * LANES : (j + 1) * LANES], dst.at[j * n : (j + 1) * n, :], packing.at[3 * c + t, j]
                 )
                 copy.start()
-                held.append(copy)
+                held[t > 0].append(copy)
             if z.used[c] < z.total[c]:
                 dst[z.used[c] :, :] = jnp.zeros((z.total[c] - z.used[c], LANES), jnp.float32)
 
@@ -198,11 +198,10 @@
     small_in = to_plane(2, lambda peer: small_plane.at[b], lambda d: small_plane.at[b])
 
     late = []
-    for c in range(2):
-        late += to_shard(3 + c, lambda peer, c=c: weights[c], fulls[c].at[rows(s, z.n[c], 8), :])
-        copy = pltpu.make_async_copy(weights[c], fulls[c].at[rows(s, z.n[c], 8), :], local.at[10 + c])
-        copy.start()
-        held.append(copy)
+    for copy in held[0]:
+        copy.wait()
+    for c in range(2):
+        late += to_shard(3 + c, lambda peer, c=c: fulls[c].at[s], fulls[c].at[s])
     late += to_shard(5, lambda peer: state.at[s], state.at[s])
 
     z_in = []
@@ -246,11 +245,11 @@
         back_plane.append(
             to_plane(3 + c, lambda peer, c=c, mine=mine: fins[c].at[mine, :], lambda d, c=c, mine=mine: fins[c].at[mine, :])
         )
-    for copy in held:
+    for copy in held[1]:
         copy.wait()
     sums[s] = jnp.zeros((z.sum_rows, LANES), jnp.float32)
     for c in range(2):
-        weight = wvs[c][...]
+        weight = fulls[c][s]
         sums[s, c * (B + 1) : c * (B + 1) + 1, :] = jnp.sum(weight * weight, axis=0, keepdims=True)
 
     def updates(c, d):
@@ -258,7 +257,7 @@
         mine = rows(index, z.quarter[c], 16)
         summed = fins[c][mine, :].astype(jnp.float32)
         _, _, update = step_math(summed, fvs[c][mine, :], svs[c][mine, :])
-        update = update + DECAY * wvs[c][mine, :]
+        update = update + DECAY * fulls[c][s, mine, :]
         sums[s, pl.ds(c * (B + 1) + 1 + index, 1), :] = jnp.sum(update * update, axis=0, keepdims=True)
         us[c][s, mine, :] = update.astype(jnp.bfloat16)
         return to_shard(
@@ -378,7 +377,7 @@
             for k in range(S):
                 own = slice(k * n, (k + 1) * n)
                 update = u[k, j * n : (j + 1) * n, :].astype(jnp.float32)
-                new[own, lanes] = (full[own, lanes] - 0.01 * ratios[c] * update).astype(jnp.bfloat16)
+                new[own, lanes] = (full[k, j * n : (j + 1) * n, :] - 0.01 * ratios[c] * update).astype(jnp.bfloat16)
 
 
 def on_device(
@@ -391,7 +390,6 @@
     z = Sizes(shards, replicas, wq.shape, wo.shape, wn.shape, wb.shape)
     S, B, A = z.S, z.B, z.A
     wn, fn, sn = (value.reshape(1, -1) for value in (wn, fn, sn))
-    any_spec = pl.BlockSpec(memory_space=pl.ANY)
     vmem = pl.BlockSpec(memory_space=pltpu.VMEM)
     shape = jax.ShapeDtypeStruct
     whole = [(n * S, cols) for n, cols in zip(z.n, z.cols)]
@@ -404,10 +402,10 @@
         functools.partial(exchange_kernel, z),
         out_shape=[shape((z.total[c], LANES), bf16) for c in both]
         + [shape((S, z.total[c], LANES), bf16) for c in both]
-        + [shape(whole[c], f32) for c in both]
+        + [shape((S, z.total[c], LANES), f32) for c in both]
         + [shape((z.small_rows, LANES), f32), shape((S, z.state_rows, LANES), f32), shape((S, z.sum_rows, LANES), f32)],
         in_specs=[pl.BlockSpec(memory_space=pltpu.HBM)] * 16,
-        out_specs=[vmem] * 4 + [any_spec] * 2 + [vmem] * 3,
+        out_specs=[vmem] * 9,
         scratch_shapes=scratch(lambda c: (S, z.n[c], z.cols[c]), f32)
         + scratch(lambda c: (z.total[c], LANES), f32)
         + scratch(lambda c: (z.total[c], LANES), bf16)
@@ -415,7 +413,7 @@
         + scratch(lambda c: (z.quarter[c], LANES), f32)
         + scratch(lambda c: (z.quarter[c], LANES), bf16)
         + scratch(lambda c: (max(A - 1, 1), z.piece[c], LANES), bf16)
-        + scratch(lambda c: (z.total[c], LANES), f32) * 3
+        + scratch(lambda c: (z.total[c], LANES), f32) * 2
         + [pltpu.VMEM((k, z.small_rows, LANES), f32) for k in (S, B, A)]
         + [pltpu.VMEM(value.shape, f32) for value in (gn, gb, wn, wb, fn, fb, sn, sb)]
         + [pltpu.SemaphoreType.DMA((7 + 2 * B, S))] * 2
@@ -438,7 +436,7 @@
         + [shape((2, 4), f32), shape((1, 4), f32)],
         in_specs=[vmem] * 13,
         out_specs=[vmem] * 14,
-        compiler_params=pltpu.CompilerParams(vmem_limit_bytes=40 * 1024 * 1024),
+        compiler_params=pltpu.CompilerParams(vmem_limit_bytes=60 * 1024 * 1024),
         name="finish",
     )(*outs, fq, fo, sq, so)
     results = list(results)

time: 48.3 us -> 34.4 us (0.71)
  local copies, waits for them, and re-layouts: 8.25 us -> 0 us
  Pallas kernels: 38.8 us -> 33.6 us
    unnamed x26 -> x0, local copies, waits for them, and re-layouts: 8.25 us -> none
    pallas_call x1, Pallas kernels: 36.9 us -> 29.3 us  [on_device(): pl.pallas_call(functools.partial(exchange_kernel, z), out_shape=[shape((z...]
    pallas_call x1, Pallas kernels: 1.9 us -> 4.29 us  [on_device(): pl.pallas_call(functools.partial(finish_kernel, z), out_shape=[shape(whol...]
where the time goes in v3:
time: 34.4 us; the launch traced here: 34.3 us
  Pallas kernels  33.6 us (98%)
  between operations  0.66 us (2%)
    pallas_call x1, Pallas kernels, on_device(): pl.pallas_call(functools.partial(exchange_kernel, z), out_shape=[shape((z...  29.3 us
    pallas_call x1, Pallas kernels, on_device(): pl.pallas_call(functools.partial(finish_kernel, z), out_shape=[shape(whol...  4.29 us

profile of v3, /device:TPU:0, one launch (start us, length us, event | category | flops | bytes accessed | tf_op | source)
XLA Modules:
  0.0 34.3 jit_solution(11277367363882827944)
XLA Ops:
  0.6 29.3 %exchange.1 = (bf16[768,128]{1,0:T(8,128)(2,1)}, bf16[768,128]{1,0:T(8,128)(2,1)}, bf16[2,768,128]{2,1,0:T(8,128)(2,1)}, bf16[2,768,128]{2,1,0:T(8,128)(2,1)}, f...) custom-call(f32[1,512,384]{2,1,0:T(8,128)} %gq.1, ...), custom_call_target="tpu_custom_call" | custom-call | tf_op jit(solution)/shard_map/exchange/pallas_call | solution.py:401
  30.0 4.3 %finish.1 = (bf16[512,384]{1,0:T(8,128)(2,1)}, bf16[384,512]{1,0:T(8,128)(2,1)}, bf16[512]{0:T(512)(128)(2,1)}, bf16[6,32]{1,0:T(8,128)(2,1)}, f32[256,384]{1,0:...) custom-call(bf16[768,128]{1,0:T(8,128)(2,1)} %get-tuple-element.37.f, ...), custom_call_target="tpu_custom_call" | custom-call | tf_op jit(solution)/shard_map/finish/pallas_call | solution.py:429

commit v4 on v3

--- a/solution.py
+++ b/solution.py
@@ -227,6 +227,14 @@
     small_in = to_z(2, lambda peer: small_z.at[a], lambda d: small_z.at[a])
 
     back_z = []
+    back_plane = [[], []]
+
+    def forward(c, d):
+        piece = rows(b * A + lax.rem(a + A - d, A), z.piece[c], 16)
+        back_plane[c].append(
+            to_plane(3 + c * A + d, lambda peer: fins[c].at[piece, :], lambda offset: fins[c].at[piece, :])
+        )
+
     for c in range(2):
         arrived(z_in[c])
         part = quarters[c][rows(a, z.piece[c], 16), :]
@@ -238,13 +246,12 @@
             to_z(3 + c, lambda peer, c=c, mine=mine: fins[c].at[mine, :], lambda d, c=c, mine=mine: fins[c].at[mine, :])
         )
 
-    back_plane = []
-    for c in range(2):
-        arrived(back_z[c])
-        mine = rows(b, z.quarter[c], 16)
-        back_plane.append(
-            to_plane(3 + c, lambda peer, c=c, mine=mine: fins[c].at[mine, :], lambda d, c=c, mine=mine: fins[c].at[mine, :])
-        )
+        forward(c, 0)
+
+    for c in range(2):
+        for d in range(1, A):
+            back_z[c][d - 1].wait_recv()
+            forward(c, d)
     for copy in held[1]:
         copy.wait()
     sums[s] = jnp.zeros((z.sum_rows, LANES), jnp.float32)
@@ -273,7 +280,8 @@
     small_out[...] = small
     for c in range(2):
         for d in range(1, B):
-            back_plane[c][d - 1].wait_recv()
+            for copies in back_plane[c]:
+                copies[d - 1].wait_recv()
             late += updates(c, d)
     late += to_shard(6 + 2 * B, lambda peer: sums.at[s], sums.at[s])
     arrived(late)
@@ -417,7 +425,7 @@
         + [pltpu.VMEM((k, z.small_rows, LANES), f32) for k in (S, B, A)]
         + [pltpu.VMEM(value.shape, f32) for value in (gn, gb, wn, wb, fn, fb, sn, sb)]
         + [pltpu.SemaphoreType.DMA((7 + 2 * B, S))] * 2
-        + [pltpu.SemaphoreType.DMA((5, B))] * 2
+        + [pltpu.SemaphoreType.DMA((3 + 2 * A, B))] * 2
         + [pltpu.SemaphoreType.DMA((5, A))] * 2
         + [pltpu.SemaphoreType.DMA((12,)), pltpu.SemaphoreType.DMA((6, max(z.blocks)))],
         compiler_params=pltpu.CompilerParams(

time: 34.4 us -> 34.6 us (level)
  no operation moved by 1% of the time
where the time goes in v4:
time: 34.6 us; the launch traced here: 34.4 us
  Pallas kernels  33.8 us (98%)
  between operations  0.66 us (2%)
    pallas_call x1, Pallas kernels, on_device(): pl.pallas_call(functools.partial(exchange_kernel, z), out_shape=[shape((z...  29.5 us
    pallas_call x1, Pallas kernels, on_device(): pl.pallas_call(functools.partial(finish_kernel, z), out_shape=[shape(whol...  4.29 us

profile of v4, /device:TPU:0, one launch (start us, length us, event | category | flops | bytes accessed | tf_op | source)
XLA Modules:
  0.0 34.4 jit_solution(12784317308309479028)
XLA Ops:
  0.6 29.5 %exchange.1 = (bf16[768,128]{1,0:T(8,128)(2,1)}, bf16[768,128]{1,0:T(8,128)(2,1)}, bf16[2,768,128]{2,1,0:T(8,128)(2,1)}, bf16[2,768,128]{2,1,0:T(8,128)(2,1)}, f...) custom-call(f32[1,512,384]{2,1,0:T(8,128)} %gq.1, ...), custom_call_target="tpu_custom_call" | custom-call | tf_op jit(solution)/shard_map/exchange/pallas_call | solution.py:409
  30.1 4.3 %finish.1 = (bf16[512,384]{1,0:T(8,128)(2,1)}, bf16[384,512]{1,0:T(8,128)(2,1)}, bf16[512]{0:T(512)(128)(2,1)}, bf16[6,32]{1,0:T(8,128)(2,1)}, f32[256,384]{1,0:...) custom-call(bf16[768,128]{1,0:T(8,128)(2,1)} %get-tuple-element.37.f, ...), custom_call_target="tpu_custom_call" | custom-call | tf_op jit(solution)/shard_map/finish/pallas_call | solution.py:437
